TPU v7x, 512 devices: a whole 4x4x16 slice. The times are simulated.
512 devices in a mesh: dp: 4 (over y_hi, core), seq: 128 (over x, y_lo, z).
Axes of the slice: x: 4, y: 4 (y_hi: 2, y_lo: 2; y = y_hi * 2 + y_lo), z: 16, core: 2. Of those that a mesh axis runs over, the one named last changes fastest.
Arguments:
- clip_frames: bfloat16 [512, 16, 128, 128], P(('dp', 'seq')), parts along dimension 0, may hold values from -6 to 6
- cotangent: bfloat16 [512, 16, 128, 128], P(('dp', 'seq')), parts along dimension 0, may hold values from -6 to 6
- spatial_weight: bfloat16 [3, 3, 16, 16], replicated, may hold values from -0.5 to 0.5
- temporal_weight: bfloat16 [3, 3, 16, 16], replicated, may hold values from -0.4375 to 0.4375
Outputs:
- block_output: bfloat16 [512, 16, 128, 128], P(('dp', 'seq')), parts along dimension 0
- clip_grad: bfloat16 [512, 16, 128, 128], P(('dp', 'seq')), parts along dimension 0
- spatial_grad: float32 [12, 3, 16, 16], P('dp'), parts along dimension 0
- temporal_grad: float32 [12, 3, 16, 16], P('dp'), parts along dimension 0
There are 4 independent parts, one for each index of `dp`. A program takes and returns all parts, laid end to end along the dimension named above; an argument that names none is the same for every part. Nothing has to cross between parts.
All inputs are finite; a program needn't handle non-finite values.
Results may differ from a plain program's by a relative error of at most 0.0071.
Values may be sent and summed in bfloat16 or wider, within the bound.
A program may use at most 64 MiB of HBM per device.

v0:
```python
import math

import jax
import jax.numpy as jnp
from jax import lax
from jax.sharding import PartitionSpec as P


def shifted(values, row_step, col_step):
    row_count = values.shape[2]
    col_count = values.shape[3]
    padded = jnp.pad(values, ((0, 0), (0, 0), (1, 1), (1, 1)))
    return padded[
        :, :, 1 + row_step : 1 + row_step + row_count, 1 + col_step : 1 + col_step + col_count
    ]


def patches_of(values, orient):
    return jnp.concatenate(
        [shifted(values, orient * (a - 1), orient * (b - 1)) for a in range(3) for b in range(3)],
        axis=1,
    )


def time_shift(values, offset):
    length = values.shape[0]
    if offset > 0:
        return jnp.concatenate([values[offset:], jnp.zeros_like(values[:offset])], axis=0)
    if offset < 0:
        return jnp.concatenate([jnp.zeros_like(values[offset:]), values[:offset]], axis=0)
    return values


def silu_slope(preact):
    sigma = jax.nn.sigmoid(preact)
    return sigma * (1.0 + preact * (1.0 - sigma))


def temporal_forward(tiles, temporal_weight):
    states = [tiles]
    for layer in range(temporal_weight.shape[0]):
        dilation = 2**layer
        current = states[-1]
        branch = current.astype(jnp.float32)
        for tap in range(3):
            branch = branch + jnp.einsum(
                "tchw,cd->tdhw",
                time_shift(current, (tap - 1) * dilation),
                temporal_weight[layer, tap],
                preferred_element_type=jnp.float32,
            )
        states.append(branch.astype(jnp.bfloat16))
    return states


def body(clip_frames, cotangent, spatial_weight, temporal_weight):
    frames_dev, channels, row_count, col_count = clip_frames.shape
    layer_count = temporal_weight.shape[0]
    factor = 1.0 / math.sqrt(frames_dev * lax.axis_size("seq") * row_count * col_count)
    patches = patches_of(clip_frames, 1)
    flat_weight = spatial_weight.reshape(9 * channels, channels)
    preact = jnp.einsum("fkhw,kd->fdhw", patches, flat_weight, preferred_element_type=jnp.float32)
    activated = jax.nn.silu(preact).astype(jnp.bfloat16)
    tiles = lax.all_to_all(activated, "seq", split_axis=2, concat_axis=0, tiled=True)
    states = temporal_forward(tiles, temporal_weight)
    block_output = lax.all_to_all(states[-1], "seq", split_axis=0, concat_axis=2, tiled=True)
    grad_tiles = lax.all_to_all(cotangent, "seq", split_axis=2, concat_axis=0, tiled=True)
    gradient = grad_tiles
    layer_terms = [None] * layer_count
    for layer in reversed(range(layer_count)):
        dilation = 2**layer
        current = states[layer]
        local_term = jnp.stack(
            [
                jnp.einsum(
                    "tchw,tdhw->cd",
                    time_shift(current, (tap - 1) * dilation),
                    gradient,
                    preferred_element_type=jnp.float32,
                )
                for tap in range(3)
            ]
        )
        layer_terms[layer] = lax.psum(local_term, "seq")
        total = gradient.astype(jnp.float32)
        for tap in range(3):
            total = total + jnp.einsum(
                "tdhw,cd->tchw",
                time_shift(gradient, -(tap - 1) * dilation),
                temporal_weight[layer, tap],
                preferred_element_type=jnp.float32,
            )
        gradient = total.astype(jnp.bfloat16)
    grad_frames = lax.all_to_all(gradient, "seq", split_axis=0, concat_axis=2, tiled=True)
    slope = (grad_frames.astype(jnp.float32) * silu_slope(preact)).astype(jnp.bfloat16)
    spatial_term = jnp.einsum(
        "fkhw,fdhw->kd", patches, slope, preferred_element_type=jnp.float32
    ).reshape(3, 3, channels, channels)
    spatial_total = lax.psum(spatial_term, "seq")
    temporal_total = jnp.stack(layer_terms)
    mixing = spatial_weight.transpose(2, 0, 1, 3).reshape(channels, 9 * channels)
    clip_grad = jnp.einsum(
        "fkhw,ck->fchw", patches_of(slope, -1), mixing, preferred_element_type=jnp.float32
    ).astype(jnp.bfloat16)
    return (block_output, clip_grad, spatial_total * factor, temporal_total * factor)


def solution(mesh):
    placed = (P(("dp", "seq"), None, None, None), P(("dp", "seq"), None, None, None), P(), P())
    return jax.shard_map(
        body,
        mesh=mesh,
        in_specs=placed,
        out_specs=(
            P(("dp", "seq"), None, None, None),
            P(("dp", "seq"), None, None, None),
            P("dp", None, None, None),
            P("dp", None, None, None),
        ),
        check_vma=False,
    )
```

profile of v0, /device:TPU:16, one launch (start us, length us, event | category | flops | bytes accessed | tf_op | source)
XLA Modules:
  0.0 781.2 jit_solution(5370593056510770013)
XLA Ops:
  0.6 1.4 copy.73
  2.0 54.3 %all_to_all.57 = bf16[1,16,128,128]{3,1,0,2:T(8,128)(2,1)S(1)} all-to-all(bf16[1,16,128,128]{3,1,0,2:T(8,128)(2,1)S(1)} %copy.73), channel_id=1, replica_groups=mesh['dp'=4,'seq'=128] {'seq'}, dimensions={2} | all-to-all | bytes 1048576 | tf_op jit(solution)/shard_map/all_to_all | solution.py:67
  56.5 1.0 convolution_bitcast_fusion.6
  57.5 0.3 fusion.18
  57.8 0.3 fusion.28
  58.0 0.1 fusion.168
  58.2 0.3 convolution_bitcast_fusion.4
  58.4 0.3 convolution_bitcast_fusion.3
  58.7 0.3 fusion.30
  59.0 0.1 fusion.167
  59.2 0.3 convolution_bitcast_fusion.1
  59.4 0.3 convolution_bitcast_fusion
  59.7 1.1 fusion.35
  60.8 6.2 all-to-all-start.3
  67.1 0.3 copy.59
  67.4 1.0 fusion.40
  68.5 0.9 fusion.41
  69.4 1.0 fusion.42
  70.4 1.0 fusion.43
  71.4 1.2 constant_dynamic-update-slice_fusion
  72.6 1.0 fusion.44
  73.6 1.1 fusion.45
  74.7 0.9 fusion.46
  75.6 1.0 fusion.47
  76.7 23.6 %all-to-all-done.3 = bf16[128,16,1,128]{3,1,2,0:T(8,128)(2,1)S(1)} async-done(((bf16[128,16,1,128]{3,1,2,0:T(8,128)(2,1)}), bf16[128,16,1,128]{3,1,2,0:T(8,128)(2,1)S(1)}, u32[]{:S(2)}, u32[]{:S(2)}) %all-to-all-start.3) | async-done | bytes 524320 | tf_op jit(solution)/shard_map/all_to_all | solution.py:94
  100.3 3.9 fusion.39
  104.3 6.7 all-to-all-start
  111.1 3.7 fusion.56
  114.8 0.2 fusion.48
  115.1 0.3 fusion.50
  115.4 0.3 fusion.51
  115.7 0.3 fusion.52
  116.0 0.3 fusion.53
  116.4 0.3 fusion.55
  116.7 0.7 fusion.36
  117.4 0.9 copy.88
  118.4 25.7 %all-to-all-done = bf16[1,16,128,128]{3,1,0,2:T(8,128)(2,1)S(1)} async-done(((bf16[1,16,128,128]{3,1,0,2:T(8,128)(2,1)}), bf16[1,16,128,128]{3,1,0,2:T(8,128)(2,1)S(1)}, u32[]{:S(2)}, u32[]{:S(2)}) %all-to-all-start) | async-done | bytes 524320 | tf_op jit(solution)/shard_map/all_to_all | solution.py:64
  144.0 0.1 slice_bitcast_fusion.1
  144.2 0.3 convolution_bitcast_fusion.24
  144.5 0.3 convolution_bitcast_fusion.14
  144.8 0.3 convolution_bitcast_fusion.15
  145.2 0.4 fusion.33
  145.5 0.1 fusion.170
  145.7 0.3 convolution_bitcast_fusion.12
  146.0 0.3 convolution_bitcast_fusion.11
  146.4 0.4 fusion.32
  146.7 0.1 fusion.169
  146.9 0.3 convolution_bitcast_fusion.9
  147.2 0.4 copy-done.5
  147.7 0.3 convolution_bitcast_fusion.8
  148.0 1.2 fusion.34
  149.2 7.3 all-to-all-start.1
  156.5 0.3 convolution_bitcast_fusion.25
  156.8 1.4 convolution_bitcast_fusion.26
  158.2 1.4 convolution_bitcast_fusion.21
  159.6 1.4 convolution_bitcast_fusion.23
  160.9 0.3 convolution_bitcast_fusion.22
  161.3 0.3 convolution_bitcast_fusion.18
  161.6 0.3 convolution_bitcast_fusion.20
  161.9 0.3 convolution_bitcast_fusion.19
  162.3 615.6 %all-reduce.14 = (f32[3,3,16,16]{3,2,0,1:T(8,128)S(1)}, f32[1,3,16,16]{3,2,0,1:T(8,128)S(1)}, f32[1,3,16,16]{3,2,0,1:T(8,128)S(1)}, f32[1,3,16,16]{3,2,0,1:T(8,128)S(1)}) all-reduce(f32[3,3,16,16]{3,2,0,1:T(8,128)S(1)} %bitcast.469, f32[1,3,16,16]{3,2,0,1:T(8,128)S(1)} %maximum_bitcast_fusion.2, ...), channel_id=1, replica_groups=mesh['dp'=4,'seq'=128] {'seq'}, use_global_device_ids=true, to_apply=%region_0.1 | all-reduce | flops 4608 | bytes 36864 | tf_op jit(solution)/shard_map/psum | solution.py:99
  777.9 0.6 copy.89
  778.5 0.6 copy.90
  779.2 2.0 copy.87
  (31 shorter events, 0.6 us)
Async XLA Ops:
  0.6 56.8 %copy-start.8 = (bf16[3,3,16,16]{3,2,1,0:T(8,128)(2,1)S(1)}, bf16[3,3,16,16]{3,2,1,0:T(8,128)(2,1)}, u32[]{:S(2)}) copy-start(bf16[3,3,16,16]{3,2,1,0:T(8,128)(2,1)} %param.7) | copy-start | bytes 13828
  59.0 8.0 %copy-start.7 = (bf16[1,16,128,128]{3,2,1,0:T(8,128)(2,1)S(1)}, bf16[1,16,128,128]{3,2,1,0:T(8,128)(2,1)}, u32[]{:S(2)}) copy-start(bf16[1,16,128,128]{3,2,1,0:T(8,128)(2,1)} %param.4) | copy-start | bytes 1572868
  60.8 39.5 %all-to-all-start.3 = ((bf16[128,16,1,128]{3,1,2,0:T(8,128)(2,1)}), bf16[128,16,1,128]{3,1,2,0:T(8,128)(2,1)S(1)}, u32[]{:S(2)}, u32[]{:S(2)}) async-start(bf16[128,16,1,128]{3,1,2,0:T(8,128)(2,1)} %fusion.35), calls=%async_computation.3 | async-start | bytes 1048576 | tf_op jit(solution)/shard_map/all_to_all | solution.py:94
  67.4 32.9 %copy-start.9 = (bf16[3,3,16,16]{3,2,1,0:T(8,128)(2,1)S(1)}, bf16[3,3,16,16]{3,2,1,0:T(8,128)(2,1)}, u32[]{:S(2)}) copy-start(bf16[3,3,16,16]{3,2,1,0:T(8,128)(2,1)} %param.6) | copy-start | bytes 13828
  104.3 39.8 %all-to-all-start = ((bf16[1,16,128,128]{3,1,0,2:T(8,128)(2,1)}), bf16[1,16,128,128]{3,1,0,2:T(8,128)(2,1)S(1)}, u32[]{:S(2)}, u32[]{:S(2)}) async-start(bf16[1,16,128,128]{3,1,0,2:T(8,128)(2,1)} %get-tuple-element.21), calls=%async_computation | async-start | bytes 1048576 | tf_op jit(solution)/shard_map/all_to_all | solution.py:64
  144.2 1.5 copy-start
  145.7 1.5 copy-start.1
  145.7 1.5 copy-start.2
  146.9 0.8 copy-start.5
  146.9 1.1 copy-start.3
  149.2 630.0 %all-to-all-start.1 = ((bf16[128,16,1,128]{3,1,2,0:T(8,128)(2,1)}), bf16[128,16,1,128]{3,1,2,0:T(8,128)(2,1)}, u32[]{:S(2)}, u32[]{:S(2)}) async-start(bf16[128,16,1,128]{3,1,2,0:T(8,128)(2,1)} %fusion.34), calls=%async_computation.1 | async-start | bytes 1048576 | tf_op jit(solution)/shard_map/all_to_all | solution.py:66
  156.5 4.8 copy-start.6
  156.5 5.1 copy-start.4
where the time goes:
time: 782 us; the launch traced here: 781 us
  blocking collectives  670 us (86%)
  waiting for transfers between devices  49.3 us (6%)
  matrix products  22.2 us (3%)
  starting transfers between devices  20.2 us (3%)
  local copies, waits for them, and re-layouts  18.5 us (2%)
    psum x1, blocking collectives, body(): spatial_total = lax.psum(spatial_term, 'seq')  616 us
    all_to_all x1, blocking collectives, body(): lax.all_to_all(cotangent, 'seq', split_axis=2, concat_axis=0, tiled=True)  54.3 us
    all_to_all x1, waiting for transfers between devices, body(): lax.all_to_all(activated, 'seq', split_axis=2, concat_axis=0, tiled=True)  25.7 us
    all_to_all x1, waiting for transfers between devices, body(): lax.all_to_all(gradient, 'seq', split_axis=0, concat_axis=2, tiled=True)  23.6 us
    unnamed x42, local copies, waits for them, and re-layouts  16.2 us
  transfers between devices with their start and end apart: 3, of which 2 were waited for; matrix products, arithmetic and copies ran while one was open for 3% of the time, Pallas kernels for 0%

commit v1 on v0

v1 whole, which is shorter than its diff:
```python
import functools
import math

import jax
import jax.numpy as jnp
from jax import lax
from jax.experimental import pallas as pl
from jax.experimental.pallas import tpu as pltpu
from jax.sharding import PartitionSpec as P

MESH = pl.DeviceIdType.MESH
F32 = jnp.float32
BF16 = jnp.bfloat16
C = 16
N = 128
SEQ = 128
Z = 16
Q = SEQ // Z
G = 16
GROUPS = N // G
PAD = 4


def iota(shape, axis):
    return lax.broadcasted_iota(jnp.int32, shape, axis)


def mm(a, b):
    return lax.dot_general(a, b, (((1,), (0,)), ((), ())), preferred_element_type=F32)


def mm_nt(a, b):
    return lax.dot_general(a, b, (((1,), (1,)), ((), ())), preferred_element_type=F32)


def one_hot(cond):
    return jnp.where(cond, 1.0, 0.0).astype(BF16)


def banded(weights, span, offsets, transposed, out_channel_major=False):
    cols = span * C
    i = iota((G * C, cols), 0)
    j = iota((G * C, cols), 1)
    si = iota((G * C, C), 0)
    sj = iota((G * C, C), 1)
    if out_channel_major:
        place = i & (G - 1)
        spread = one_hot((si >> 4) == sj)
    else:
        place = i >> 4
        spread = one_hot((si & (C - 1)) == sj)
    tile = one_hot(iota((C, cols), 0) == (iota((C, cols), 1) & (C - 1)))
    diff = (j >> 4) - place
    total = jnp.zeros((G * C, cols), F32)
    for weight, offset in zip(weights, offsets):
        rows = (mm if transposed else mm_nt)(spread, weight).astype(BF16)
        total = jnp.where(diff == offset, mm(rows, tile), total)
    return total.astype(BF16)


def fold(acc, span, offset):
    rows = span * C
    diff = (iota((rows, G * C), 0) >> 4) - (iota((rows, G * C), 1) >> 4)
    kept = jnp.where(diff == offset, acc, 0.0)
    total = jnp.sum(kept.reshape(span, C, G * C), axis=0)
    total = total[:, :128] + total[:, 128:]
    for step in (64, 32, 16):
        total = total + pltpu.roll(total, step, 1)
    return total


def kernel(
    factor,
    clip_hbm, cot_hbm, sw_ref, tw_ref,
    out_hbm, grad_hbm, sgrad_ref, tgrad_ref,
    clip_in, cot_in, cot_f, act_f, xs, preact, bands_s, bands_v, bands_f, bands_b,
    back3, back2, back1, back0, st0, st1, st2, st3, grad_f, out_f, slopes,
    acc_t, acc_s, pack, sum1, part1, sum2, part2, sum3, out_v, grad_v,
    local_sem, send_sem, recv_sem,
):
    me = lax.axis_index("seq")
    q, z = me // Z, lax.rem(me, Z)

    cot_load = pltpu.make_async_copy(cot_hbm.at[0], cot_in, local_sem.at[0])
    cot_load.start()
    clip_load = pltpu.make_async_copy(clip_hbm.at[0], clip_in, local_sem.at[1])
    clip_load.start()

    barrier = pltpu.get_barrier_semaphore()

    @pl.loop(1, SEQ)
    def _(d):
        pl.semaphore_signal(barrier, inc=1, device_id={"seq": lax.rem(me + d, SEQ)}, device_id_type=MESH)

    def send_all(index, src, dst, at):
        def copy(k, j):
            t = lax.rem(q + k, Q) * Z + lax.rem(z + j, Z)
            return pltpu.make_async_remote_copy(
                src_ref=src.at[t], dst_ref=dst.at[at], send_sem=send_sem.at[index], recv_sem=recv_sem.at[index],
                device_id={"seq": t}, device_id_type=MESH,
            )

        @pl.loop(1, SEQ)
        def _(d):
            copy(d // Z, lax.rem(d, Z)).start()

    def wait_all(sem, ref):
        part = ref.at[pl.ds(0, SEQ - 1)]
        pltpu.make_async_copy(part, part, sem).wait()

    i = iota((G * C, G * C), 0)
    j = iota((G * C, G * C), 1)
    swap = one_hot(((i & (C - 1)) == (j >> 4)) & ((i >> 4) == (j & (G - 1))))

    cot_load.wait()

    @pl.loop(0, GROUPS)
    def _(g):
        rows = pl.ds(pl.multiple_of(g * G, G), G)
        cot_f[rows] = mm(swap, cot_in[:, rows, :].reshape(C * G, N)).astype(BF16).reshape(G, C, N)

    pl.semaphore_wait(barrier, SEQ - 1)
    send_all(0, cot_f, back3, me + PAD)
    back3[me + PAD] = cot_f[me]

    clip_load.wait()
    for b in range(3):
        bands_s[b] = banded([sw_ref[a, b] for a in range(3)], G + 2, range(3), False)
        xs[b, 0] = jnp.zeros((C, N), BF16)
        xs[b, N + 1] = jnp.zeros((C, N), BF16)
    lane = iota((G * C, N), 1)

    @pl.loop(0, GROUPS)
    def _(g):
        rows = pl.ds(pl.multiple_of(g * G, G), G)
        x = mm(swap, clip_in[:, rows, :].reshape(C * G, N))
        padded = pl.ds(g * G + 1, G)
        xs[0, padded] = jnp.where(lane == 0, 0.0, pltpu.roll(x, 1, 1)).astype(BF16).reshape(G, C, N)
        xs[1, padded] = x.astype(BF16).reshape(G, C, N)
        xs[2, padded] = jnp.where(lane == N - 1, 0.0, pltpu.roll(x, N - 1, 1)).astype(BF16).reshape(G, C, N)

    @pl.loop(0, GROUPS)
    def _(g):
        p = jnp.zeros((G * C, N), F32)
        for b in range(3):
            p = p + mm(bands_s[b], xs[b, pl.ds(g * G, G + 2)].reshape((G + 2) * C, N))
        rows = pl.ds(g * G, G)
        preact[rows] = p.reshape(G, C, N)
        act_f[rows] = (p / (1.0 + jnp.exp(-p))).astype(BF16).reshape(G, C, N)

    send_all(1, act_f, st0, me + PAD)
    st0[me + PAD] = act_f[me]

    zeros = jnp.zeros((PAD, C, N), BF16)
    for ref in (back3, back2, back1, st0, st1, st2):
        ref[pl.ds(0, PAD)] = zeros
        ref[pl.ds(N + PAD, PAD)] = zeros
    for layer in range(3):
        e = 2**layer
        span = G + 2 * e
        taps = [tw_ref[layer, k] for k in range(3)]
        bands_b[layer, :, pl.ds(0, span * C)] = banded(taps, span, [(2 - k) * e for k in range(3)], True)
        bands_f[layer, :, pl.ds(0, span * C)] = banded(taps, span, [k * e for k in range(3)], False)

    def temporal(src, dst, bands, layer, pad):
        e = 2**layer
        span = G + 2 * e

        @pl.loop(0, GROUPS)
        def _(g):
            own = src[pl.ds(g * G + PAD, G)].reshape(G * C, N).astype(F32)
            wide = src[pl.ds(g * G + PAD - e, span)].reshape(span * C, N)
            new = own + mm(bands[layer, :, pl.ds(0, span * C)], wide)
            dst[pl.ds(g * G + pad, G)] = new.astype(BF16).reshape(G, C, N)

    wait_all(recv_sem.at[0], back3)
    temporal(back3, back2, bands_b, 2, PAD)
    temporal(back2, back1, bands_b, 1, PAD)
    temporal(back1, back0, bands_b, 0, 0)
    send_all(2, back0, grad_f, me)
    grad_f[me] = back0[me]
    for b in range(3):
        bands_v[b] = banded([sw_ref[a, b] for a in range(3)], G + 2, [2 - a for a in range(3)], True, True)
        slopes[b, 0] = jnp.zeros((C, N), BF16)
        slopes[b, N + 1] = jnp.zeros((C, N), BF16)

    wait_all(recv_sem.at[1], st0)
    temporal(st0, st1, bands_f, 0, PAD)
    temporal(st1, st2, bands_f, 1, PAD)
    temporal(st2, st3, bands_f, 2, 0)
    send_all(3, st3, out_f, me)
    out_f[me] = st3[me]

    block = iota((C, 128), 1) >> 4
    last = jnp.zeros((C, 128), F32)
    packed = jnp.zeros((C, 128), F32)
    for layer, (state, back) in enumerate(((st0, back1), (st1, back2), (st2, back3))):
        e = 2**layer
        span = G + 2 * e
        acc_t[...] = jnp.zeros_like(acc_t)

        @pl.loop(0, GROUPS)
        def _(g):
            wide = state[pl.ds(g * G + PAD - e, span)].reshape(span * C, N)
            own = back[pl.ds(g * G + PAD, G)].reshape(G * C, N)
            acc_t[pl.ds(0, span * C)] += mm_nt(wide, own)

        for k in range(3):
            folded = fold(acc_t[pl.ds(0, span * C)], span, k * e)
            if layer * 3 + k < 8:
                packed = jnp.where(block == layer * 3 + k, folded, packed)
            else:
                last = jnp.where(block == 1, folded, last)
    pack[pl.ds(2, 2)] = packed.reshape(2, 8, 128)

    wait_all(recv_sem.at[2], grad_f)

    @pl.loop(0, GROUPS)
    def _(g):
        rows = pl.ds(g * G, G)
        p = preact[rows].reshape(G * C, N)
        s = 1.0 / (1.0 + jnp.exp(-p))
        slope = grad_f[rows].reshape(G * C, N).astype(F32) * (s * (1.0 + p * (1.0 - s)))
        padded = pl.ds(g * G + 1, G)
        slopes[0, padded] = jnp.where(lane == N - 1, 0.0, pltpu.roll(slope, N - 1, 1)).astype(BF16).reshape(G, C, N)
        slopes[1, padded] = slope.astype(BF16).reshape(G, C, N)
        slopes[2, padded] = jnp.where(lane == 0, 0.0, pltpu.roll(slope, 1, 1)).astype(BF16).reshape(G, C, N)

    acc_s[...] = jnp.zeros_like(acc_s)

    @pl.loop(0, GROUPS)
    def _(g):
        own = slopes[1, pl.ds(g * G + 1, G)].reshape(G * C, N)
        for b in range(3):
            acc_s[b] += mm_nt(xs[b, pl.ds(g * G, G + 2)].reshape((G + 2) * C, N), own)

    packed = jnp.zeros((C, 128), F32)
    for b in range(3):
        for a in range(3):
            folded = fold(acc_s[b], G + 2, a)
            if a * 3 + b < 8:
                packed = jnp.where(block == a * 3 + b, folded, packed)
            else:
                last = jnp.where(block == 0, folded, last)
    pack[pl.ds(0, 2)] = packed.reshape(2, 8, 128)
    pack[pl.ds(4, 2)] = last.reshape(2, 8, 128)
    pack[pl.ds(6, 2)] = jnp.zeros((2, 8, 128), F32)

    def to_columns(src_of, dst, index):
        for d in range(1, Q):
            other = lax.rem(q + d, Q)
            pltpu.make_async_remote_copy(
                src_ref=src_of(other), dst_ref=dst.at[q], send_sem=send_sem.at[index], recv_sem=recv_sem.at[index],
                device_id={"seq": other * Z + z}, device_id_type=MESH,
            ).start()

    def wait_some(sem, ref, count):
        part = ref.at[pl.ds(0, count)]
        pltpu.make_async_copy(part, part, sem).wait()

    to_columns(lambda other: pack.at[other], sum1, 4)
    sum1[q] = pack[q]

    def clip_gradient(g):
        total = jnp.zeros((C * G, N), F32)
        for b in range(3):
            total = total + mm(bands_v[b], slopes[b, pl.ds(g * G, G + 2)].reshape((G + 2) * C, N))
        grad_v[:, pl.ds(pl.multiple_of(g * G, G), G), :] = total.astype(BF16).reshape(C, G, N)

    wait_some(recv_sem.at[4], sum1, Q - 1)
    part1[...] = jnp.sum(sum1[...], axis=0)
    for d in range(1, Z):
        other = lax.rem(z + d, Z)
        pltpu.make_async_remote_copy(
            src_ref=part1, dst_ref=sum2.at[z], send_sem=send_sem.at[5], recv_sem=recv_sem.at[5],
            device_id={"seq": q * Z + other}, device_id_type=MESH,
        ).start()
    sum2[z] = part1[...]

    @pl.loop(0, GROUPS)
    def _(g):
        clip_gradient(g)

    grad_store = pltpu.make_async_copy(grad_v, grad_hbm.at[0], local_sem.at[0])
    grad_store.start()

    wait_some(recv_sem.at[5], sum2, Z - 1)
    part2[...] = jnp.sum(sum2[...], axis=0)
    to_columns(lambda other: part2, sum3, 6)
    sum3[q] = part2[...]
    wait_some(recv_sem.at[6], sum3, Q - 1)

    spatial = sum3[pl.ds(0, 2)].reshape(C, 128) * factor
    temporal_sum = sum3[pl.ds(2, 2)].reshape(C, 128) * factor
    last = sum3[pl.ds(4, 2)].reshape(C, 128) * factor
    for tap in range(9):
        at = (128 - tap * C) % 128
        from_s, at_s = (spatial, at) if tap < 8 else (last, 0)
        from_t, at_t = (temporal_sum, at) if tap < 8 else (last, 128 - C)
        sgrad_ref[tap // 3, tap % 3] = pltpu.roll(from_s, at_s, 1)[:, :C]
        tgrad_ref[tap // 3, tap % 3] = pltpu.roll(from_t, at_t, 1)[:, :C]

    wait_all(recv_sem.at[3], out_f)

    @pl.loop(0, GROUPS)
    def _(g):
        rows = pl.ds(pl.multiple_of(g * G, G), G)
        out_v[:, rows, :] = mm(swap, out_f[rows].reshape(G * C, N)).astype(BF16).reshape(C, G, N)

    out_store = pltpu.make_async_copy(out_v, out_hbm.at[0], local_sem.at[1])
    out_store.start()

    for index, ref in enumerate((cot_f, act_f, back0, st3)):
        wait_all(send_sem.at[index], ref)
    wait_some(send_sem.at[4], sum1, Q - 1)
    wait_some(send_sem.at[5], sum2, Z - 1)
    wait_some(send_sem.at[6], sum3, Q - 1)
    grad_store.wait()
    out_store.wait()


def body(clip_frames, cotangent, spatial_weight, temporal_weight):
    factor = 1.0 / math.sqrt(N * N * N)
    vmem = pl.BlockSpec(memory_space=pltpu.VMEM)
    anywhere = pl.BlockSpec(memory_space=pl.ANY)
    frame = pltpu.VMEM((N, C, N), BF16)
    padded = pltpu.VMEM((N + 2 * PAD, C, N), BF16)
    return pl.pallas_call(
        functools.partial(kernel, factor),
        out_shape=(
            jax.ShapeDtypeStruct((1, C, N, N), BF16),
            jax.ShapeDtypeStruct((1, C, N, N), BF16),
            jax.ShapeDtypeStruct((3, 3, C, C), F32),
            jax.ShapeDtypeStruct((3, 3, C, C), F32),
        ),
        in_specs=[anywhere, anywhere, vmem, vmem],
        out_specs=(anywhere, anywhere, vmem, vmem),
        scratch_shapes=[
            pltpu.VMEM((C, N, N), BF16),
            pltpu.VMEM((C, N, N), BF16),
            frame,
            frame,
            pltpu.VMEM((3, N + 2, C, N), BF16),
            pltpu.VMEM((N, C, N), F32),
            pltpu.VMEM((3, G * C, (G + 2) * C), BF16),
            pltpu.VMEM((3, G * C, (G + 2) * C), BF16),
            pltpu.VMEM((3, G * C, (G + 8) * C), BF16),
            pltpu.VMEM((3, G * C, (G + 8) * C), BF16),
            padded, padded, padded, frame,
            padded, padded, padded, frame,
            frame,
            frame,
            pltpu.VMEM((3, N + 2, C, N), BF16),
            pltpu.VMEM(((G + 8) * C, G * C), F32),
            pltpu.VMEM((3, (G + 2) * C, G * C), F32),
            pltpu.VMEM((Q, 8, 128), F32),
            pltpu.VMEM((Q, 8, 128), F32),
            pltpu.VMEM((8, 128), F32),
            pltpu.VMEM((Z, 8, 128), F32),
            pltpu.VMEM((8, 128), F32),
            pltpu.VMEM((Q, 8, 128), F32),
            pltpu.VMEM((C, N, N), BF16),
            pltpu.VMEM((C, N, N), BF16),
            pltpu.SemaphoreType.DMA((2,)),
            pltpu.SemaphoreType.DMA((7,)),
            pltpu.SemaphoreType.DMA((7,)),
        ],
        compiler_params=pltpu.CompilerParams(collective_id=0, has_side_effects=True, vmem_limit_bytes=40 << 20),
    )(clip_frames, cotangent, spatial_weight, temporal_weight)


def solution(mesh):
    placed = (P(("dp", "seq"), None, None, None), P(("dp", "seq"), None, None, None), P(), P())
    return jax.shard_map(
        body,
        mesh=mesh,
        in_specs=placed,
        out_specs=(
            P(("dp", "seq"), None, None, None),
            P(("dp", "seq"), None, None, None),
            P("dp", None, None, None),
            P("dp", None, None, None),
        ),
        check_vma=False,
    )
```

time: 782 us -> 127 us (0.16)
  the two profiles are of different devices: /device:TPU:16 before, /device:TPU:24 now
where the time goes in v1:
time: 127 us; the launch traced here: 126 us
  Pallas kernels  119 us (94%)
  local copies, waits for them, and re-layouts  6.46 us (5%)
    pallas_call x1, Pallas kernels, body(): pl.pallas_call(functools.partial(kernel, factor), out_shape=(jax.ShapeDty...  119 us
    unnamed x12, local copies, waits for them, and re-layouts  6.46 us

profile of v1, /device:TPU:24, one launch (start us, length us, event | category | flops | bytes accessed | tf_op | source)
XLA Modules:
  0.0 126.4 jit_solution(11375274966309516193)
XLA Ops:
  0.6 0.0 copy-start
  0.6 1.0 copy-done
  1.7 0.0 copy-start.1
  1.7 1.0 copy-done.1
  2.7 0.0 copy-start.2
  2.7 0.8 copy-done.2
  3.5 0.0 copy-start.3
  3.5 0.8 copy-done.3
  4.3 119.3 %shard_map.75 = (bf16[1,16,128,128]{3,2,1,0:T(8,128)(2,1)S(1)}, bf16[1,16,128,128]{3,2,1,0:T(8,128)(2,1)S(1)}, f32[3,3,16,16]{3,2,1,0:T(8,128)S(1)}, f32[3,3,16,16]{3,2,1,0:T(8,128)S(1)}) custom-call(bf16[1,16,128,128]{3,2,1,0:T(8,128)(2,1)S(1)} %copy-done, bf16[1,16,128,128]{3,2,1,0:T(8,128)(2,1)S(1)} %copy-done.1, bf16[3,3,16,16]{3,2,1,0:T(8,128)(2,1)S(1)} %copy-done.2, ...), custom_call_target="tpu_custom_call" | custom-call | tf_op jit(solution)/shard_map/pallas_call | solution.py:328
  123.6 0.8 copy.12
  124.4 0.8 copy.13
  125.2 0.6 copy.14
  125.8 0.6 copy.15
Async XLA Ops:
  0.6 1.0 copy-start
  1.7 1.0 copy-start.1
  2.7 0.8 copy-start.2
  3.5 0.8 copy-start.3

commit v2 on v1

--- a/solution.py
+++ b/solution.py
@@ -19,6 +19,8 @@
 G = 16
 GROUPS = N // G
 PAD = 4
+PIECE = 5
+VMEM_LIMIT = 60 << 20
 
 
 def iota(shape, axis):
@@ -71,12 +73,12 @@
 
 def kernel(
     factor,
-    clip_hbm, cot_hbm, sw_ref, tw_ref,
+    clip_hbm, cot_hbm, sw_hbm, tw_hbm,
     out_hbm, grad_hbm, sgrad_ref, tgrad_ref,
-    clip_in, cot_in, cot_f, act_f, xs, preact, bands_s, bands_v, bands_f, bands_b,
+    sw_ref, tw_ref, clip_in, cot_in, cot_f, act_f, xs, preact, bands_s, bands_v, bands_f, bands_b,
     back3, back2, back1, back0, st0, st1, st2, st3, grad_f, out_f, slopes,
-    acc_t, acc_s, pack, sum1, part1, sum2, part2, sum3, out_v, grad_v,
-    local_sem, send_sem, recv_sem,
+    acc_t, acc_s, pack, sum1, part1, sum2, part2, sum3, total, out_v, grad_v,
+    local_sem, send_sem, recv_sem, send_out, recv_grad, recv_out, ready,
 ):
     me = lax.axis_index("seq")
     q, z = me // Z, lax.rem(me, Z)
@@ -85,28 +87,51 @@
     cot_load.start()
     clip_load = pltpu.make_async_copy(clip_hbm.at[0], clip_in, local_sem.at[1])
     clip_load.start()
+    sw_load = pltpu.make_async_copy(sw_hbm, sw_ref, local_sem.at[2])
+    sw_load.start()
+    tw_load = pltpu.make_async_copy(tw_hbm, tw_ref, local_sem.at[3])
+    tw_load.start()
 
     barrier = pltpu.get_barrier_semaphore()
-
-    @pl.loop(1, SEQ)
-    def _(d):
-        pl.semaphore_signal(barrier, inc=1, device_id={"seq": lax.rem(me + d, SEQ)}, device_id_type=MESH)
+    for d in range(1, Q):
+        pl.semaphore_signal(barrier, inc=1, device_id={"seq": lax.rem(q + d, Q) * Z + z}, device_id_type=MESH)
+    for d in range(1, Z):
+        pl.semaphore_signal(barrier, inc=1, device_id={"seq": q * Z + lax.rem(z + d, Z)}, device_id_type=MESH)
+
+    def send_group(k, src, dst, at, sent, received):
+        column = lax.rem(q + k, Q) * Z
+
+        def send(i):
+            j = 8 + lax.rem(i, 2) * (i + 1) // 2 - (1 - lax.rem(i, 2)) * (i // 2)
+            t = column + lax.rem(z + j, Z)
+            pltpu.make_async_remote_copy(
+                src_ref=src.at[t], dst_ref=dst.at[at], send_sem=sent, recv_sem=received,
+                device_id={"seq": t}, device_id_type=MESH,
+            ).start()
+
+        @pl.loop(0, Z if k else Z - 1)
+        def _(i):
+            send(i)
 
     def send_all(index, src, dst, at):
-        def copy(k, j):
-            t = lax.rem(q + k, Q) * Z + lax.rem(z + j, Z)
-            return pltpu.make_async_remote_copy(
-                src_ref=src.at[t], dst_ref=dst.at[at], send_sem=send_sem.at[index], recv_sem=recv_sem.at[index],
-                device_id={"seq": t}, device_id_type=MESH,
-            )
-
-        @pl.loop(1, SEQ)
-        def _(d):
-            copy(d // Z, lax.rem(d, Z)).start()
+        for k in range(Q):
+            send_group(k, src, dst, at, send_sem.at[index], recv_sem.at[index])
+
+    def wait_some(sem, ref, count):
+        part = ref.at[pl.ds(0, count)]
+        pltpu.make_async_copy(part, part, sem).wait()
 
     def wait_all(sem, ref):
-        part = ref.at[pl.ds(0, SEQ - 1)]
-        pltpu.make_async_copy(part, part, sem).wait()
+        wait_some(sem, ref, SEQ - 1)
+
+    def wait_group(sem, ref, k):
+        @pl.when(k == 0)
+        def _():
+            wait_some(sem, ref, Z - 1)
+
+        @pl.when(k > 0)
+        def _():
+            wait_some(sem, ref, Z)
 
     i = iota((G * C, G * C), 0)
     j = iota((G * C, G * C), 1)
@@ -114,16 +139,28 @@
 
     cot_load.wait()
 
-    @pl.loop(0, GROUPS)
-    def _(g):
-        rows = pl.ds(pl.multiple_of(g * G, G), G)
+    def cotangent_rows(k):
+        rows = pl.ds(pl.multiple_of(lax.rem(q + k, Q) * G, G), G)
         cot_f[rows] = mm(swap, cot_in[:, rows, :].reshape(C * G, N)).astype(BF16).reshape(G, C, N)
 
-    pl.semaphore_wait(barrier, SEQ - 1)
-    send_all(0, cot_f, back3, me + PAD)
+    cotangent_rows(0)
+    pl.semaphore_wait(barrier, Q - 1 + Z - 1)
+    for d in range(1, Z):
+        pl.semaphore_signal(ready, inc=1, device_id={"seq": q * Z + lax.rem(z + d, Z)}, device_id_type=MESH)
+    send_group(0, cot_f, back3, me + PAD, send_sem.at[0], recv_sem.at[0])
     back3[me + PAD] = cot_f[me]
 
+    @pl.loop(1, Q)
+    def _(k):
+        cotangent_rows(k)
+
+    pl.semaphore_wait(ready, Z - 1)
+    for k in range(1, Q):
+        send_group(k, cot_f, back3, me + PAD, send_sem.at[0], recv_sem.at[0])
+
     clip_load.wait()
+    sw_load.wait()
+    tw_load.wait()
     for b in range(3):
         bands_s[b] = banded([sw_ref[a, b] for a in range(3)], G + 2, range(3), False)
         xs[b, 0] = jnp.zeros((C, N), BF16)
@@ -177,7 +214,8 @@
     temporal(back3, back2, bands_b, 2, PAD)
     temporal(back2, back1, bands_b, 1, PAD)
     temporal(back1, back0, bands_b, 0, 0)
-    send_all(2, back0, grad_f, me)
+    for k in range(Q):
+        send_group(k, back0, grad_f, me, send_sem.at[2], recv_grad.at[k])
     grad_f[me] = back0[me]
     for b in range(3):
         bands_v[b] = banded([sw_ref[a, b] for a in range(3)], G + 2, [2 - a for a in range(3)], True, True)
@@ -188,7 +226,14 @@
     temporal(st0, st1, bands_f, 0, PAD)
     temporal(st1, st2, bands_f, 1, PAD)
     temporal(st2, st3, bands_f, 2, 0)
-    send_all(3, st3, out_f, me)
+
+    def send_output(k):
+        if k >= 3:
+            wait_some(send_out.at[k - 3], st3, Z if k > 3 else Z - 1)
+        send_group(k, st3, out_f, me, send_out.at[k], recv_out.at[k])
+
+    for k in range(3):
+        send_output(k)
     out_f[me] = st3[me]
 
     block = iota((C, 128), 1) >> 4
@@ -210,41 +255,43 @@
             if layer * 3 + k < 8:
                 packed = jnp.where(block == layer * 3 + k, folded, packed)
             else:
-                last = jnp.where(block == 1, folded, last)
-    pack[pl.ds(2, 2)] = packed.reshape(2, 8, 128)
-
-    wait_all(recv_sem.at[2], grad_f)
+                last = jnp.where((block & 1) == 1, folded, last)
+    packed_t = packed
+
+    acc_s[...] = jnp.zeros_like(acc_s)
 
     @pl.loop(0, GROUPS)
-    def _(g):
+    def _(k):
+        wait_group(recv_grad.at[k], grad_f, k)
+        g = lax.rem(q + Q - k, Q)
         rows = pl.ds(g * G, G)
         p = preact[rows].reshape(G * C, N)
         s = 1.0 / (1.0 + jnp.exp(-p))
         slope = grad_f[rows].reshape(G * C, N).astype(F32) * (s * (1.0 + p * (1.0 - s)))
+        own = slope.astype(BF16)
         padded = pl.ds(g * G + 1, G)
         slopes[0, padded] = jnp.where(lane == N - 1, 0.0, pltpu.roll(slope, N - 1, 1)).astype(BF16).reshape(G, C, N)
-        slopes[1, padded] = slope.astype(BF16).reshape(G, C, N)
+        slopes[1, padded] = own.reshape(G, C, N)
         slopes[2, padded] = jnp.where(lane == 0, 0.0, pltpu.roll(slope, 1, 1)).astype(BF16).reshape(G, C, N)
-
-    acc_s[...] = jnp.zeros_like(acc_s)
-
-    @pl.loop(0, GROUPS)
-    def _(g):
-        own = slopes[1, pl.ds(g * G + 1, G)].reshape(G * C, N)
         for b in range(3):
             acc_s[b] += mm_nt(xs[b, pl.ds(g * G, G + 2)].reshape((G + 2) * C, N), own)
 
-    packed = jnp.zeros((C, 128), F32)
+    packed_s = jnp.zeros((C, 128), F32)
     for b in range(3):
         for a in range(3):
             folded = fold(acc_s[b], G + 2, a)
             if a * 3 + b < 8:
-                packed = jnp.where(block == a * 3 + b, folded, packed)
+                packed_s = jnp.where(block == a * 3 + b, folded, packed_s)
             else:
-                last = jnp.where(block == 0, folded, last)
-    pack[pl.ds(0, 2)] = packed.reshape(2, 8, 128)
-    pack[pl.ds(4, 2)] = last.reshape(2, 8, 128)
-    pack[pl.ds(6, 2)] = jnp.zeros((2, 8, 128), F32)
+                last = jnp.where((block & 1) == 0, folded, last)
+    packed_l = jnp.zeros((4, 128), F32)
+    for m in range(4):
+        packed_l = jnp.where((block[:4] >> 1) == m, last[4 * m : 4 * m + 4], packed_l)
+    for m in range(4):
+        pack[m, :4] = packed_s[4 * m : 4 * m + 4]
+        pack[m, 4:] = packed_l[m : m + 1]
+        pack[m + 4, :4] = packed_t[4 * m : 4 * m + 4]
+        pack[m + 4, 4:] = jnp.zeros((1, 128), F32)
 
     def to_columns(src_of, dst, index):
         for d in range(1, Q):
@@ -254,78 +301,105 @@
                 device_id={"seq": other * Z + z}, device_id_type=MESH,
             ).start()
 
-    def wait_some(sem, ref, count):
-        part = ref.at[pl.ds(0, count)]
-        pltpu.make_async_copy(part, part, sem).wait()
-
-    to_columns(lambda other: pack.at[other], sum1, 4)
-    sum1[q] = pack[q]
-
     def clip_gradient(g):
         total = jnp.zeros((C * G, N), F32)
         for b in range(3):
             total = total + mm(bands_v[b], slopes[b, pl.ds(g * G, G + 2)].reshape((G + 2) * C, N))
         grad_v[:, pl.ds(pl.multiple_of(g * G, G), G), :] = total.astype(BF16).reshape(C, G, N)
 
-    wait_some(recv_sem.at[4], sum1, Q - 1)
+    to_columns(lambda other: pack.at[other], sum1, 3)
+    sum1[q] = pack[q]
+    send_output(3)
+
+    @pl.loop(0, GROUPS // 2)
+    def _(g):
+        clip_gradient(g)
+
+    wait_some(recv_sem.at[3], sum1, Q - 1)
     part1[...] = jnp.sum(sum1[...], axis=0)
     for d in range(1, Z):
         other = lax.rem(z + d, Z)
         pltpu.make_async_remote_copy(
-            src_ref=part1, dst_ref=sum2.at[z], send_sem=send_sem.at[5], recv_sem=recv_sem.at[5],
+            src_ref=part1, dst_ref=sum2.at[z], send_sem=send_sem.at[4], recv_sem=recv_sem.at[4],
             device_id={"seq": q * Z + other}, device_id_type=MESH,
         ).start()
     sum2[z] = part1[...]
-
-    @pl.loop(0, GROUPS)
+    send_output(4)
+    send_output(5)
+
+    @pl.loop(GROUPS // 2, GROUPS)
     def _(g):
         clip_gradient(g)
 
     grad_store = pltpu.make_async_copy(grad_v, grad_hbm.at[0], local_sem.at[0])
     grad_store.start()
-
-    wait_some(recv_sem.at[5], sum2, Z - 1)
+    send_output(6)
+
+    wait_some(recv_sem.at[4], sum2, Z - 1)
     part2[...] = jnp.sum(sum2[...], axis=0)
-    to_columns(lambda other: part2, sum3, 6)
+    to_columns(lambda other: part2, sum3, 5)
     sum3[q] = part2[...]
-    wait_some(recv_sem.at[6], sum3, Q - 1)
-
-    spatial = sum3[pl.ds(0, 2)].reshape(C, 128) * factor
-    temporal_sum = sum3[pl.ds(2, 2)].reshape(C, 128) * factor
-    last = sum3[pl.ds(4, 2)].reshape(C, 128) * factor
+    send_output(7)
+
+    def output_rows(k):
+        wait_group(recv_out.at[k], out_f, k)
+        rows = pl.ds(pl.multiple_of(lax.rem(q + Q - k, Q) * G, G), G)
+        out_v[:, rows, :] = mm(swap, out_f[rows].reshape(G * C, N)).astype(BF16).reshape(C, G, N)
+        pltpu.make_async_copy(out_v.at[:, rows, :], out_hbm.at[0, :, rows, :], local_sem.at[1]).start()
+
+    @pl.loop(0, GROUPS // 2)
+    def _(k):
+        output_rows(k)
+
+    wait_some(recv_sem.at[5], sum3, Q - 1)
+    for m in range(4):
+        total[pl.ds(4 * m, 4)] = sum3[m, :4] * factor
+        total[pl.ds(16 + 4 * m, 4)] = sum3[m + 4, :4] * factor
+        total[pl.ds(32 + m, 1)] = sum3[m, 4:] * factor
+    last = total[pl.ds(32, 4)]
     for tap in range(9):
         at = (128 - tap * C) % 128
-        from_s, at_s = (spatial, at) if tap < 8 else (last, 0)
-        from_t, at_t = (temporal_sum, at) if tap < 8 else (last, 128 - C)
-        sgrad_ref[tap // 3, tap % 3] = pltpu.roll(from_s, at_s, 1)[:, :C]
-        tgrad_ref[tap // 3, tap % 3] = pltpu.roll(from_t, at_t, 1)[:, :C]
-
-    wait_all(recv_sem.at[3], out_f)
-
-    @pl.loop(0, GROUPS)
-    def _(g):
-        rows = pl.ds(pl.multiple_of(g * G, G), G)
-        out_v[:, rows, :] = mm(swap, out_f[rows].reshape(G * C, N)).astype(BF16).reshape(C, G, N)
-
-    out_store = pltpu.make_async_copy(out_v, out_hbm.at[0], local_sem.at[1])
-    out_store.start()
-
-    for index, ref in enumerate((cot_f, act_f, back0, st3)):
+        if tap < 8:
+            sgrad_ref[tap // 3, tap % 3] = pltpu.roll(total[pl.ds(0, C)], at, 1)[:, :C] if at else total[pl.ds(0, C)][:, :C]
+            tgrad_ref[tap // 3, tap % 3] = pltpu.roll(total[pl.ds(C, C)], at, 1)[:, :C] if at else total[pl.ds(C, C)][:, :C]
+        else:
+            for m in range(4):
+                back_by = (128 - 32 * m) % 128
+                sgrad_ref[2, 2, pl.ds(4 * m, 4)] = (pltpu.roll(last, back_by, 1) if back_by else last)[:, :C]
+                tgrad_ref[2, 2, pl.ds(4 * m, 4)] = pltpu.roll(last, back_by - C if m else 128 - C, 1)[:, :C]
+
+    @pl.loop(GROUPS // 2, GROUPS)
+    def _(k):
+        output_rows(k)
+
+    for index, ref in enumerate((cot_f, act_f, back0)):
         wait_all(send_sem.at[index], ref)
-    wait_some(send_sem.at[4], sum1, Q - 1)
-    wait_some(send_sem.at[5], sum2, Z - 1)
-    wait_some(send_sem.at[6], sum3, Q - 1)
+    for k in range(5, Q):
+        wait_some(send_out.at[k], st3, Z)
+    wait_some(send_sem.at[3], sum1, Q - 1)
+    wait_some(send_sem.at[4], sum2, Z - 1)
+    wait_some(send_sem.at[5], sum3, Q - 1)
     grad_store.wait()
-    out_store.wait()
+    pltpu.make_async_copy(out_v, out_hbm.at[0], local_sem.at[1]).wait()
+
+
+def hand_over(*refs):
+    count = (len(refs) - 1) // 2
+    sems = refs[-1]
+    copies = [pltpu.make_async_copy(refs[n], refs[count + n], sems.at[n]) for n in range(count)]
+    for copy in copies:
+        copy.start()
+    for copy in copies:
+        copy.wait()
 
 
 def body(clip_frames, cotangent, spatial_weight, temporal_weight):
     factor = 1.0 / math.sqrt(N * N * N)
     vmem = pl.BlockSpec(memory_space=pltpu.VMEM)
-    anywhere = pl.BlockSpec(memory_space=pl.ANY)
+    anywhere = pl.BlockSpec(memory_space=pltpu.HBM)
     frame = pltpu.VMEM((N, C, N), BF16)
     padded = pltpu.VMEM((N + 2 * PAD, C, N), BF16)
-    return pl.pallas_call(
+    results = pl.pallas_call(
         functools.partial(kernel, factor),
         out_shape=(
             jax.ShapeDtypeStruct((1, C, N, N), BF16),
@@ -333,9 +407,11 @@
             jax.ShapeDtypeStruct((3, 3, C, C), F32),
             jax.ShapeDtypeStruct((3, 3, C, C), F32),
         ),
-        in_specs=[anywhere, anywhere, vmem, vmem],
+        in_specs=[anywhere] * 4,
         out_specs=(anywhere, anywhere, vmem, vmem),
         scratch_shapes=[
+            pltpu.VMEM((3, 3, C, C), BF16),
+            pltpu.VMEM((3, 3, C, C), BF16),
             pltpu.VMEM((C, N, N), BF16),
             pltpu.VMEM((C, N, N), BF16),
             frame,
@@ -353,20 +429,33 @@
             pltpu.VMEM((3, N + 2, C, N), BF16),
             pltpu.VMEM(((G + 8) * C, G * C), F32),
             pltpu.VMEM((3, (G + 2) * C, G * C), F32),
-            pltpu.VMEM((Q, 8, 128), F32),
-            pltpu.VMEM((Q, 8, 128), F32),
-            pltpu.VMEM((8, 128), F32),
-            pltpu.VMEM((Z, 8, 128), F32),
-            pltpu.VMEM((8, 128), F32),
-            pltpu.VMEM((Q, 8, 128), F32),
+            pltpu.VMEM((Q, PIECE, 128), F32),
+            pltpu.VMEM((Q, PIECE, 128), F32),
+            pltpu.VMEM((PIECE, 128), F32),
+            pltpu.VMEM((Z, PIECE, 128), F32),
+            pltpu.VMEM((PIECE, 128), F32),
+            pltpu.VMEM((Q, PIECE, 128), F32),
+            pltpu.VMEM((40, 128), F32),
             pltpu.VMEM((C, N, N), BF16),
             pltpu.VMEM((C, N, N), BF16),
-            pltpu.SemaphoreType.DMA((2,)),
-            pltpu.SemaphoreType.DMA((7,)),
-            pltpu.SemaphoreType.DMA((7,)),
+            pltpu.SemaphoreType.DMA((4,)),
+            pltpu.SemaphoreType.DMA((6,)),
+            pltpu.SemaphoreType.DMA((6,)),
+            pltpu.SemaphoreType.DMA((Q,)),
+            pltpu.SemaphoreType.DMA((Q,)),
+            pltpu.SemaphoreType.DMA((Q,)),
+            pltpu.SemaphoreType.REGULAR,
         ],
-        compiler_params=pltpu.CompilerParams(collective_id=0, has_side_effects=True, vmem_limit_bytes=40 << 20),
+        compiler_params=pltpu.CompilerParams(collective_id=0, has_side_effects=True, vmem_limit_bytes=VMEM_LIMIT),
     )(clip_frames, cotangent, spatial_weight, temporal_weight)
+    return pl.pallas_call(
+        hand_over,
+        out_shape=tuple(jax.ShapeDtypeStruct(r.shape, r.dtype) for r in results),
+        in_specs=[anywhere] * 4,
+        out_specs=(anywhere,) * 4,
+        scratch_shapes=[pltpu.SemaphoreType.DMA((4,))],
+        compiler_params=pltpu.CompilerParams(vmem_limit_bytes=VMEM_LIMIT),
+    )(*results)
 
 
 def solution(mesh):

time: 127 us -> 154 us (1.21)
  Pallas kernels: 119 us -> 153 us
  local copies, waits for them, and re-layouts: 6.46 us -> 0 us
    pallas_call x0 -> x1, Pallas kernels: none -> 37.4 us  [body(): pl.pallas_call(hand_over, out_shape=tuple((jax.ShapeDtypeStruct(r.shape,...]
    unnamed x12 -> x0, local copies, waits for them, and re-layouts: 6.46 us -> none
    pallas_call x1, Pallas kernels: 119 us -> 116 us  [body(): pl.pallas_call(functools.partial(kernel, factor), out_shape=(jax.ShapeDty...]
where the time goes in v2:
time: 154 us
  Pallas kernels  153 us (99%)
    pallas_call x1, Pallas kernels, body(): pl.pallas_call(functools.partial(kernel, factor), out_shape=(jax.ShapeDty...  116 us
    pallas_call x1, Pallas kernels, body(): pl.pallas_call(hand_over, out_shape=tuple((jax.ShapeDtypeStruct(r.shape,...  37.4 us

profile of v2, /device:TPU:24, one launch (start us, length us, event | category | flops | bytes accessed | tf_op | source)
XLA Modules:
  0.0 154.0 jit_solution(16235077818218803403)
XLA Ops:
  0.6 116.0 %shard_map.75 = (bf16[1,16,128,128]{3,2,1,0:T(8,128)(2,1)}, bf16[1,16,128,128]{3,2,1,0:T(8,128)(2,1)}, f32[3,3,16,16]{3,2,1,0:T(8,128)}, f32[3,3,16,16]{3,2,1,0:T(8,128)}) custom-call(bf16[1,16,128,128]{3,2,1,0:T(8,128)(2,1)} %clip_hbm.1, bf16[1,16,128,128]{3,2,1,0:T(8,128)(2,1)} %cot_hbm.1, bf16[3,3,16,16]{3,2,1,0:T(8,128)(2,1)} %sw_hbm.1, ...), custom_call_target="tpu_custom_call" | custom-call | tf_op jit(solution)/shard_map/pallas_call | solution.py:402
  116.7 37.4 %shard_map.76 = (bf16[1,16,128,128]{3,2,1,0:T(8,128)(2,1)}, bf16[1,16,128,128]{3,2,1,0:T(8,128)(2,1)}, f32[3,3,16,16]{3,2,1,0:T(8,128)}, f32[3,3,16,16]{3,2,1,0:T(8,128)}) custom-call(bf16[1,16,128,128]{3,2,1,0:T(8,128)(2,1)} %get-tuple-element.8.refs_0_, bf16[1,16,128,128]{3,2,1,0:T(8,128)(2,1)} %get-tuple-element.9.refs_1_, ...), custom_call_target="tpu_custom_call" | custom-call | tf_op jit(solution)/shard_map/pallas_call | solution.py:451

commit v3 on v2

--- a/solution.py
+++ b/solution.py
@@ -21,6 +21,7 @@
 PAD = 4
 PIECE = 5
 VMEM_LIMIT = 60 << 20
+HANDED = 4
 
 
 def iota(shape, axis):
@@ -383,14 +384,22 @@
     pltpu.make_async_copy(out_v, out_hbm.at[0], local_sem.at[1]).wait()
 
 
-def hand_over(*refs):
-    count = (len(refs) - 1) // 2
-    sems = refs[-1]
-    copies = [pltpu.make_async_copy(refs[n], refs[count + n], sems.at[n]) for n in range(count)]
-    for copy in copies:
-        copy.start()
-    for copy in copies:
-        copy.wait()
+def hand_over(out_in, grad_in, sgrad_in, tgrad_in, out_hbm, grad_hbm, sgrad_hbm, tgrad_hbm, *scratch):
+    stages, load_sem, store_sem = scratch[:4], scratch[4], scratch[5]
+    loads, stores = [], []
+    pairs = zip((out_in, grad_in, sgrad_in, tgrad_in), stages, (out_hbm, grad_hbm, sgrad_hbm, tgrad_hbm))
+    for source, stage, target in pairs:
+        for part in range(HANDED if source.shape[0] == 1 else 1):
+            at = (0, pl.ds(part * C // HANDED, C // HANDED)) if source.shape[0] == 1 else slice(None)
+            loads.append(pltpu.make_async_copy(source.at[at], stage.at[at], load_sem.at[len(loads)]))
+            stores.append(pltpu.make_async_copy(stage.at[at], target.at[at], store_sem.at[len(stores)]))
+    for load in loads:
+        load.start()
+    for load, store in zip(loads, stores):
+        load.wait()
+        store.start()
+    for store in stores:
+        store.wait()
 
 
 def body(clip_frames, cotangent, spatial_weight, temporal_weight):
@@ -453,7 +462,7 @@
         out_shape=tuple(jax.ShapeDtypeStruct(r.shape, r.dtype) for r in results),
         in_specs=[anywhere] * 4,
         out_specs=(anywhere,) * 4,
-        scratch_shapes=[pltpu.SemaphoreType.DMA((4,))],
+        scratch_shapes=[pltpu.VMEM(r.shape, r.dtype) for r in results] + [pltpu.SemaphoreType.DMA((2 * HANDED + 2,))] * 2,
         compiler_params=pltpu.CompilerParams(vmem_limit_bytes=VMEM_LIMIT),
     )(*results)
 

time: 154 us -> 119 us (0.77)
  Pallas kernels: 153 us -> 118 us
    pallas_call x1, Pallas kernels: 37.4 us -> 2.17 us  [body(): pl.pallas_call(hand_over, out_shape=tuple((jax.ShapeDtypeStruct(r.shape,...]
where the time goes in v3:
time: 119 us
  Pallas kernels  118 us (99%)
    pallas_call x1, Pallas kernels, body(): pl.pallas_call(functools.partial(kernel, factor), out_shape=(jax.ShapeDty...  116 us

profile of v3, /device:TPU:24, one launch (start us, length us, event | category | flops | bytes accessed | tf_op | source)
XLA Modules:
  0.0 118.8 jit_solution(7554124569560254381)
XLA Ops:
  0.6 116.0 %shard_map.75 = (bf16[1,16,128,128]{3,2,1,0:T(8,128)(2,1)}, bf16[1,16,128,128]{3,2,1,0:T(8,128)(2,1)}, f32[3,3,16,16]{3,2,1,0:T(8,128)}, f32[3,3,16,16]{3,2,1,0:T(8,128)}) custom-call(bf16[1,16,128,128]{3,2,1,0:T(8,128)(2,1)} %clip_hbm.1, bf16[1,16,128,128]{3,2,1,0:T(8,128)(2,1)} %cot_hbm.1, bf16[3,3,16,16]{3,2,1,0:T(8,128)(2,1)} %sw_hbm.1, ...), custom_call_target="tpu_custom_call" | custom-call | tf_op jit(solution)/shard_map/pallas_call | solution.py:411
  116.7 2.2 %shard_map.76 = (bf16[1,16,128,128]{3,2,1,0:T(8,128)(2,1)}, bf16[1,16,128,128]{3,2,1,0:T(8,128)(2,1)}, f32[3,3,16,16]{3,2,1,0:T(8,128)}, f32[3,3,16,16]{3,2,1,0:T(8,128)}) custom-call(bf16[1,16,128,128]{3,2,1,0:T(8,128)(2,1)} %get-tuple-element.8.out_in, bf16[1,16,128,128]{3,2,1,0:T(8,128)(2,1)} %get-tuple-element.9.grad_in, ...), custom_call_target="tpu_custom_call" | custom-call | tf_op jit(solution)/shard_map/pallas_call | solution.py:460

commit v4 on v3

--- a/solution.py
+++ b/solution.py
@@ -76,10 +76,10 @@
     factor,
     clip_hbm, cot_hbm, sw_hbm, tw_hbm,
     out_hbm, grad_hbm, sgrad_ref, tgrad_ref,
-    sw_ref, tw_ref, clip_in, cot_in, cot_f, act_f, xs, preact, bands_s, bands_v, bands_f, bands_b,
+    sw_ref, tw_ref, clip_in, cot_in, cot_f, cot_z, act_f, xs, preact, bands_s, bands_v, bands_f, bands_b,
     back3, back2, back1, back0, st0, st1, st2, st3, grad_f, out_f, slopes,
     acc_t, acc_s, pack, sum1, part1, sum2, part2, sum3, total, out_v, grad_v,
-    local_sem, send_sem, recv_sem, send_out, recv_grad, recv_out, ready,
+    local_sem, send_sem, recv_sem, send_act, send_out, recv_grad, recv_out, ready,
 ):
     me = lax.axis_index("seq")
     q, z = me // Z, lax.rem(me, Z)
@@ -114,10 +114,6 @@
         def _(i):
             send(i)
 
-    def send_all(index, src, dst, at):
-        for k in range(Q):
-            send_group(k, src, dst, at, send_sem.at[index], recv_sem.at[index])
-
     def wait_some(sem, ref, count):
         part = ref.at[pl.ds(0, count)]
         pltpu.make_async_copy(part, part, sem).wait()
@@ -140,24 +136,24 @@
 
     cot_load.wait()
 
-    def cotangent_rows(k):
-        rows = pl.ds(pl.multiple_of(lax.rem(q + k, Q) * G, G), G)
-        cot_f[rows] = mm(swap, cot_in[:, rows, :].reshape(C * G, N)).astype(BF16).reshape(G, C, N)
-
-    cotangent_rows(0)
+    @pl.loop(0, GROUPS)
+    def _(g):
+        rows = pl.ds(pl.multiple_of(g * G, G), G)
+        cot_f[g] = mm(swap, cot_in[:, rows, :].reshape(C * G, N)).astype(BF16).reshape(G, C, N)
+
     pl.semaphore_wait(barrier, Q - 1 + Z - 1)
+
+    @pl.loop(1, Z)
+    def _(d):
+        other = lax.rem(z + d, Z)
+        pltpu.make_async_remote_copy(
+            src_ref=cot_f.at[:, other], dst_ref=cot_z.at[z], send_sem=send_sem.at[0], recv_sem=recv_sem.at[0],
+            device_id={"seq": q * Z + other}, device_id_type=MESH,
+        ).start()
+
     for d in range(1, Z):
         pl.semaphore_signal(ready, inc=1, device_id={"seq": q * Z + lax.rem(z + d, Z)}, device_id_type=MESH)
-    send_group(0, cot_f, back3, me + PAD, send_sem.at[0], recv_sem.at[0])
-    back3[me + PAD] = cot_f[me]
-
-    @pl.loop(1, Q)
-    def _(k):
-        cotangent_rows(k)
-
-    pl.semaphore_wait(ready, Z - 1)
-    for k in range(1, Q):
-        send_group(k, cot_f, back3, me + PAD, send_sem.at[0], recv_sem.at[0])
+    cot_z[z] = cot_f[:, z]
 
     clip_load.wait()
     sw_load.wait()
@@ -186,7 +182,15 @@
         preact[rows] = p.reshape(G, C, N)
         act_f[rows] = (p / (1.0 + jnp.exp(-p))).astype(BF16).reshape(G, C, N)
 
-    send_all(1, act_f, st0, me + PAD)
+    pl.semaphore_wait(ready, Z - 1)
+
+    def send_activated(k):
+        if k >= 3:
+            wait_some(send_act.at[k - 3], act_f, Z if k > 3 else Z - 1)
+        send_group(k, act_f, st0, me + PAD, send_act.at[k], recv_sem.at[1])
+
+    for k in range(3):
+        send_activated(k)
     st0[me + PAD] = act_f[me]
 
     zeros = jnp.zeros((PAD, C, N), BF16)
@@ -211,12 +215,24 @@
             new = own + mm(bands[layer, :, pl.ds(0, span * C)], wide)
             dst[pl.ds(g * G + pad, G)] = new.astype(BF16).reshape(G, C, N)
 
-    wait_all(recv_sem.at[0], back3)
+    wait_some(recv_sem.at[0], cot_z, Z - 1)
+    own_frames = pl.ds(q * Z + PAD, Z)
+    for k in range(1, Q):
+        other = lax.rem(q + k, Q)
+        pltpu.make_async_remote_copy(
+            src_ref=cot_z.at[:, other], dst_ref=back3.at[own_frames], send_sem=send_sem.at[2], recv_sem=recv_sem.at[2],
+            device_id={"seq": other * Z + z}, device_id_type=MESH,
+        ).start()
+    back3[own_frames] = cot_z[:, q]
+    for k in range(3, Q):
+        send_activated(k)
+
+    wait_some(recv_sem.at[2], back3, SEQ - Z)
     temporal(back3, back2, bands_b, 2, PAD)
     temporal(back2, back1, bands_b, 1, PAD)
     temporal(back1, back0, bands_b, 0, 0)
     for k in range(Q):
-        send_group(k, back0, grad_f, me, send_sem.at[2], recv_grad.at[k])
+        send_group(k, back0, grad_f, me, send_sem.at[1], recv_grad.at[k])
     grad_f[me] = back0[me]
     for b in range(3):
         bands_v[b] = banded([sw_ref[a, b] for a in range(3)], G + 2, [2 - a for a in range(3)], True, True)
@@ -373,9 +389,11 @@
     def _(k):
         output_rows(k)
 
-    for index, ref in enumerate((cot_f, act_f, back0)):
-        wait_all(send_sem.at[index], ref)
+    wait_some(send_sem.at[0], cot_z, Z - 1)
+    wait_all(send_sem.at[1], back0)
+    wait_some(send_sem.at[2], back3, SEQ - Z)
     for k in range(5, Q):
+        wait_some(send_act.at[k], act_f, Z)
         wait_some(send_out.at[k], st3, Z)
     wait_some(send_sem.at[3], sum1, Q - 1)
     wait_some(send_sem.at[4], sum2, Z - 1)
@@ -423,7 +441,8 @@
             pltpu.VMEM((3, 3, C, C), BF16),
             pltpu.VMEM((C, N, N), BF16),
             pltpu.VMEM((C, N, N), BF16),
-            frame,
+            pltpu.VMEM((Q, Z, C, N), BF16),
+            pltpu.VMEM((Z, Q, C, N), BF16),
             frame,
             pltpu.VMEM((3, N + 2, C, N), BF16),
             pltpu.VMEM((N, C, N), F32),
@@ -453,6 +472,7 @@
             pltpu.SemaphoreType.DMA((Q,)),
             pltpu.SemaphoreType.DMA((Q,)),
             pltpu.SemaphoreType.DMA((Q,)),
+            pltpu.SemaphoreType.DMA((Q,)),
             pltpu.SemaphoreType.REGULAR,
         ],
         compiler_params=pltpu.CompilerParams(collective_id=0, has_side_effects=True, vmem_limit_bytes=VMEM_LIMIT),

time: 119 us -> 117 us (0.983)
  Pallas kernels: 118 us -> 116 us
    pallas_call x1, Pallas kernels: 116 us -> 114 us  [body(): pl.pallas_call(functools.partial(kernel, factor), out_shape=(jax.ShapeDty...]
where the time goes in v4:
time: 117 us
  Pallas kernels  116 us (99%)
    pallas_call x1, Pallas kernels, body(): pl.pallas_call(functools.partial(kernel, factor), out_shape=(jax.ShapeDty...  114 us

profile of v4, /device:TPU:24, one launch (start us, length us, event | category | flops | bytes accessed | tf_op | source)
XLA Modules:
  0.0 116.8 jit_solution(17136813318440797415)
XLA Ops:
  0.6 114.0 %shard_map.75 = (bf16[1,16,128,128]{3,2,1,0:T(8,128)(2,1)}, bf16[1,16,128,128]{3,2,1,0:T(8,128)(2,1)}, f32[3,3,16,16]{3,2,1,0:T(8,128)}, f32[3,3,16,16]{3,2,1,0:T(8,128)}) custom-call(bf16[1,16,128,128]{3,2,1,0:T(8,128)(2,1)} %clip_hbm.1, bf16[1,16,128,128]{3,2,1,0:T(8,128)(2,1)} %cot_hbm.1, bf16[3,3,16,16]{3,2,1,0:T(8,128)(2,1)} %sw_hbm.1, ...), custom_call_target="tpu_custom_call" | custom-call | tf_op jit(solution)/shard_map/pallas_call | solution.py:429
  114.7 2.2 %shard_map.76 = (bf16[1,16,128,128]{3,2,1,0:T(8,128)(2,1)}, bf16[1,16,128,128]{3,2,1,0:T(8,128)(2,1)}, f32[3,3,16,16]{3,2,1,0:T(8,128)}, f32[3,3,16,16]{3,2,1,0:T(8,128)}) custom-call(bf16[1,16,128,128]{3,2,1,0:T(8,128)(2,1)} %get-tuple-element.8.out_in, bf16[1,16,128,128]{3,2,1,0:T(8,128)(2,1)} %get-tuple-element.9.grad_in, ...), custom_call_target="tpu_custom_call" | custom-call | tf_op jit(solution)/shard_map/pallas_call | solution.py:480

commit v5 on v4

--- a/solution.py
+++ b/solution.py
@@ -19,7 +19,8 @@
 G = 16
 GROUPS = N // G
 PAD = 4
-PIECE = 5
+PIECES = 2 * Q
+PIECE = 3
 VMEM_LIMIT = 60 << 20
 HANDED = 4
 
@@ -75,8 +76,8 @@
 def kernel(
     factor,
     clip_hbm, cot_hbm, sw_hbm, tw_hbm,
-    out_hbm, grad_hbm, sgrad_ref, tgrad_ref,
-    sw_ref, tw_ref, clip_in, cot_in, cot_f, cot_z, act_f, xs, preact, bands_s, bands_v, bands_f, bands_b,
+    out_hbm, grad_hbm, sgrad_hbm, tgrad_hbm,
+    sw_ref, tw_ref, sgrad_ref, tgrad_ref, clip_in, cot_in, cot_f, cot_z, act_f, xs, preact, bands_s, bands_v, bands_f, bands_b,
     back3, back2, back1, back0, st0, st1, st2, st3, grad_f, out_f, slopes,
     acc_t, acc_s, pack, sum1, part1, sum2, part2, sum3, total, out_v, grad_v,
     local_sem, send_sem, recv_sem, send_act, send_out, recv_grad, recv_out, ready,
@@ -249,7 +250,7 @@
             wait_some(send_out.at[k - 3], st3, Z if k > 3 else Z - 1)
         send_group(k, st3, out_f, me, send_out.at[k], recv_out.at[k])
 
-    for k in range(3):
+    for k in range(2):
         send_output(k)
     out_f[me] = st3[me]
 
@@ -304,18 +305,22 @@
     packed_l = jnp.zeros((4, 128), F32)
     for m in range(4):
         packed_l = jnp.where((block[:4] >> 1) == m, last[4 * m : 4 * m + 4], packed_l)
-    for m in range(4):
-        pack[m, :4] = packed_s[4 * m : 4 * m + 4]
-        pack[m, 4:] = packed_l[m : m + 1]
-        pack[m + 4, :4] = packed_t[4 * m : 4 * m + 4]
-        pack[m + 4, 4:] = jnp.zeros((1, 128), F32)
-
-    def to_columns(src_of, dst, index):
-        for d in range(1, Q):
-            other = lax.rem(q + d, Q)
+    for m in range(PIECES // 2):
+        pack[m, :2] = packed_s[2 * m : 2 * m + 2]
+        pack[m + 8, :2] = packed_t[2 * m : 2 * m + 2]
+        pack[m, 2:] = packed_l[m : m + 1] if m < 4 else jnp.zeros((1, 128), F32)
+        pack[m + 8, 2:] = jnp.zeros((1, 128), F32)
+
+    piece = q * 2 + lax.rem(z, 2)
+    pair = z // 2
+
+    def to_group(src_of, dst, index):
+        @pl.loop(1, PIECES)
+        def _(d):
+            other = lax.rem(piece + d, PIECES)
             pltpu.make_async_remote_copy(
-                src_ref=src_of(other), dst_ref=dst.at[q], send_sem=send_sem.at[index], recv_sem=recv_sem.at[index],
-                device_id={"seq": other * Z + z}, device_id_type=MESH,
+                src_ref=src_of(other), dst_ref=dst.at[piece], send_sem=send_sem.at[index], recv_sem=recv_sem.at[index],
+                device_id={"seq": (other // 2) * Z + pair * 2 + lax.rem(other, 2)}, device_id_type=MESH,
             ).start()
 
     def clip_gradient(g):
@@ -324,23 +329,24 @@
             total = total + mm(bands_v[b], slopes[b, pl.ds(g * G, G + 2)].reshape((G + 2) * C, N))
         grad_v[:, pl.ds(pl.multiple_of(g * G, G), G), :] = total.astype(BF16).reshape(C, G, N)
 
-    to_columns(lambda other: pack.at[other], sum1, 3)
-    sum1[q] = pack[q]
+    to_group(lambda other: pack.at[other], sum1, 3)
+    sum1[piece] = pack[piece]
+    send_output(2)
     send_output(3)
 
     @pl.loop(0, GROUPS // 2)
     def _(g):
         clip_gradient(g)
 
-    wait_some(recv_sem.at[3], sum1, Q - 1)
+    wait_some(recv_sem.at[3], sum1, PIECES - 1)
     part1[...] = jnp.sum(sum1[...], axis=0)
-    for d in range(1, Z):
-        other = lax.rem(z + d, Z)
+    for d in range(1, Z // 2):
+        other = lax.rem(z + 2 * d, Z)
         pltpu.make_async_remote_copy(
-            src_ref=part1, dst_ref=sum2.at[z], send_sem=send_sem.at[4], recv_sem=recv_sem.at[4],
+            src_ref=part1, dst_ref=sum2.at[pair], send_sem=send_sem.at[4], recv_sem=recv_sem.at[4],
             device_id={"seq": q * Z + other}, device_id_type=MESH,
         ).start()
-    sum2[z] = part1[...]
+    sum2[pair] = part1[...]
     send_output(4)
     send_output(5)
 
@@ -352,10 +358,10 @@
     grad_store.start()
     send_output(6)
 
-    wait_some(recv_sem.at[4], sum2, Z - 1)
+    wait_some(recv_sem.at[4], sum2, Z // 2 - 1)
     part2[...] = jnp.sum(sum2[...], axis=0)
-    to_columns(lambda other: part2, sum3, 5)
-    sum3[q] = part2[...]
+    to_group(lambda other: part2, sum3, 5)
+    sum3[piece] = part2[...]
     send_output(7)
 
     def output_rows(k):
@@ -364,15 +370,15 @@
         out_v[:, rows, :] = mm(swap, out_f[rows].reshape(G * C, N)).astype(BF16).reshape(C, G, N)
         pltpu.make_async_copy(out_v.at[:, rows, :], out_hbm.at[0, :, rows, :], local_sem.at[1]).start()
 
-    @pl.loop(0, GROUPS // 2)
+    @pl.loop(0, GROUPS - 1)
     def _(k):
         output_rows(k)
 
-    wait_some(recv_sem.at[5], sum3, Q - 1)
+    wait_some(recv_sem.at[5], sum3, PIECES - 1)
+    for m in range(PIECES):
+        total[pl.ds(2 * m, 2)] = sum3[m, :2] * factor
     for m in range(4):
-        total[pl.ds(4 * m, 4)] = sum3[m, :4] * factor
-        total[pl.ds(16 + 4 * m, 4)] = sum3[m + 4, :4] * factor
-        total[pl.ds(32 + m, 1)] = sum3[m, 4:] * factor
+        total[pl.ds(32 + m, 1)] = sum3[m, 2:] * factor
     last = total[pl.ds(32, 4)]
     for tap in range(9):
         at = (128 - tap * C) % 128
@@ -385,9 +391,14 @@
                 sgrad_ref[2, 2, pl.ds(4 * m, 4)] = (pltpu.roll(last, back_by, 1) if back_by else last)[:, :C]
                 tgrad_ref[2, 2, pl.ds(4 * m, 4)] = pltpu.roll(last, back_by - C if m else 128 - C, 1)[:, :C]
 
-    @pl.loop(GROUPS // 2, GROUPS)
-    def _(k):
-        output_rows(k)
+    small_stores = [
+        pltpu.make_async_copy(sgrad_ref, sgrad_hbm, local_sem.at[2]),
+        pltpu.make_async_copy(tgrad_ref, tgrad_hbm, local_sem.at[3]),
+    ]
+    for store in small_stores:
+        store.start()
+
+    output_rows(GROUPS - 1)
 
     wait_some(send_sem.at[0], cot_z, Z - 1)
     wait_all(send_sem.at[1], back0)
@@ -395,9 +406,11 @@
     for k in range(5, Q):
         wait_some(send_act.at[k], act_f, Z)
         wait_some(send_out.at[k], st3, Z)
-    wait_some(send_sem.at[3], sum1, Q - 1)
-    wait_some(send_sem.at[4], sum2, Z - 1)
-    wait_some(send_sem.at[5], sum3, Q - 1)
+    wait_some(send_sem.at[3], sum1, PIECES - 1)
+    wait_some(send_sem.at[4], sum2, Z // 2 - 1)
+    wait_some(send_sem.at[5], sum3, PIECES - 1)
+    for store in small_stores:
+        store.wait()
     grad_store.wait()
     pltpu.make_async_copy(out_v, out_hbm.at[0], local_sem.at[1]).wait()
 
@@ -422,7 +435,6 @@
 
 def body(clip_frames, cotangent, spatial_weight, temporal_weight):
     factor = 1.0 / math.sqrt(N * N * N)
-    vmem = pl.BlockSpec(memory_space=pltpu.VMEM)
     anywhere = pl.BlockSpec(memory_space=pltpu.HBM)
     frame = pltpu.VMEM((N, C, N), BF16)
     padded = pltpu.VMEM((N + 2 * PAD, C, N), BF16)
@@ -435,10 +447,12 @@
             jax.ShapeDtypeStruct((3, 3, C, C), F32),
         ),
         in_specs=[anywhere] * 4,
-        out_specs=(anywhere, anywhere, vmem, vmem),
+        out_specs=(anywhere,) * 4,
         scratch_shapes=[
             pltpu.VMEM((3, 3, C, C), BF16),
             pltpu.VMEM((3, 3, C, C), BF16),
+            pltpu.VMEM((3, 3, C, C), F32),
+            pltpu.VMEM((3, 3, C, C), F32),
             pltpu.VMEM((C, N, N), BF16),
             pltpu.VMEM((C, N, N), BF16),
             pltpu.VMEM((Q, Z, C, N), BF16),
@@ -457,12 +471,12 @@
             pltpu.VMEM((3, N + 2, C, N), BF16),
             pltpu.VMEM(((G + 8) * C, G * C), F32),
             pltpu.VMEM((3, (G + 2) * C, G * C), F32),
-            pltpu.VMEM((Q, PIECE, 128), F32),
-            pltpu.VMEM((Q, PIECE, 128), F32),
+            pltpu.VMEM((PIECES, PIECE, 128), F32),
+            pltpu.VMEM((PIECES, PIECE, 128), F32),
             pltpu.VMEM((PIECE, 128), F32),
-            pltpu.VMEM((Z, PIECE, 128), F32),
+            pltpu.VMEM((Z // 2, PIECE, 128), F32),
             pltpu.VMEM((PIECE, 128), F32),
-            pltpu.VMEM((Q, PIECE, 128), F32),
+            pltpu.VMEM((PIECES, PIECE, 128), F32),
             pltpu.VMEM((40, 128), F32),
             pltpu.VMEM((C, N, N), BF16),
             pltpu.VMEM((C, N, N), BF16),

time: 117 us -> 117 us (level); the launches traced: 117 us -> 115 us
  Pallas kernels: 116 us -> 114 us
    pallas_call x1, Pallas kernels: 114 us -> 112 us  [body(): pl.pallas_call(functools.partial(kernel, factor), out_shape=(jax.ShapeDty...]
where the time goes in v5:
time: 117 us; the launch traced here: 115 us
  Pallas kernels  114 us (97%)
    pallas_call x1, Pallas kernels, body(): pl.pallas_call(functools.partial(kernel, factor), out_shape=(jax.ShapeDty...  112 us

profile of v5, /device:TPU:24, one launch (start us, length us, event | category | flops | bytes accessed | tf_op | source)
XLA Modules:
  0.0 114.8 jit_solution(10571127937744560037)
XLA Ops:
  0.6 112.0 %shard_map.75 = (bf16[1,16,128,128]{3,2,1,0:T(8,128)(2,1)}, bf16[1,16,128,128]{3,2,1,0:T(8,128)(2,1)}, f32[3,3,16,16]{3,2,1,0:T(8,128)}, f32[3,3,16,16]{3,2,1,0:T(8,128)}) custom-call(bf16[1,16,128,128]{3,2,1,0:T(8,128)(2,1)} %clip_hbm.1, bf16[1,16,128,128]{3,2,1,0:T(8,128)(2,1)} %cot_hbm.1, bf16[3,3,16,16]{3,2,1,0:T(8,128)(2,1)} %sw_hbm.1, ...), custom_call_target="tpu_custom_call" | custom-call | tf_op jit(solution)/shard_map/pallas_call | solution.py:441
  112.6 2.2 %shard_map.76 = (bf16[1,16,128,128]{3,2,1,0:T(8,128)(2,1)}, bf16[1,16,128,128]{3,2,1,0:T(8,128)(2,1)}, f32[3,3,16,16]{3,2,1,0:T(8,128)}, f32[3,3,16,16]{3,2,1,0:T(8,128)}) custom-call(bf16[1,16,128,128]{3,2,1,0:T(8,128)(2,1)} %get-tuple-element.8.out_in, bf16[1,16,128,128]{3,2,1,0:T(8,128)(2,1)} %get-tuple-element.9.grad_in, ...), custom_call_target="tpu_custom_call" | custom-call | tf_op jit(solution)/shard_map/pallas_call | solution.py:494

commit v6 on v5

--- a/solution.py
+++ b/solution.py
@@ -357,12 +357,12 @@
     grad_store = pltpu.make_async_copy(grad_v, grad_hbm.at[0], local_sem.at[0])
     grad_store.start()
     send_output(6)
+    send_output(7)
 
     wait_some(recv_sem.at[4], sum2, Z // 2 - 1)
     part2[...] = jnp.sum(sum2[...], axis=0)
     to_group(lambda other: part2, sum3, 5)
     sum3[piece] = part2[...]
-    send_output(7)
 
     def output_rows(k):
         wait_group(recv_out.at[k], out_f, k)

time: 117 us -> 115 us (0.983); the launches traced: 115 us -> 114 us
  no operation moved by 1% of the time
where the time goes in v6:
time: 115 us; the launch traced here: 114 us
  Pallas kernels  114 us (99%)
    pallas_call x1, Pallas kernels, body(): pl.pallas_call(functools.partial(kernel, factor), out_shape=(jax.ShapeDty...  112 us

profile of v6, /device:TPU:24, one launch (start us, length us, event | category | flops | bytes accessed | tf_op | source)
XLA Modules:
  0.0 114.5 jit_solution(11196809088989859193)
XLA Ops:
  0.6 111.6 %shard_map.75 = (bf16[1,16,128,128]{3,2,1,0:T(8,128)(2,1)}, bf16[1,16,128,128]{3,2,1,0:T(8,128)(2,1)}, f32[3,3,16,16]{3,2,1,0:T(8,128)}, f32[3,3,16,16]{3,2,1,0:T(8,128)}) custom-call(bf16[1,16,128,128]{3,2,1,0:T(8,128)(2,1)} %clip_hbm.1, bf16[1,16,128,128]{3,2,1,0:T(8,128)(2,1)} %cot_hbm.1, bf16[3,3,16,16]{3,2,1,0:T(8,128)(2,1)} %sw_hbm.1, ...), custom_call_target="tpu_custom_call" | custom-call | tf_op jit(solution)/shard_map/pallas_call | solution.py:441
  112.3 2.2 %shard_map.76 = (bf16[1,16,128,128]{3,2,1,0:T(8,128)(2,1)}, bf16[1,16,128,128]{3,2,1,0:T(8,128)(2,1)}, f32[3,3,16,16]{3,2,1,0:T(8,128)}, f32[3,3,16,16]{3,2,1,0:T(8,128)}) custom-call(bf16[1,16,128,128]{3,2,1,0:T(8,128)(2,1)} %get-tuple-element.8.out_in, bf16[1,16,128,128]{3,2,1,0:T(8,128)(2,1)} %get-tuple-element.9.grad_in, ...), custom_call_target="tpu_custom_call" | custom-call | tf_op jit(solution)/shard_map/pallas_call | solution.py:494

commit v7 on v6

--- a/solution.py
+++ b/solution.py
@@ -22,7 +22,7 @@
 PIECES = 2 * Q
 PIECE = 3
 VMEM_LIMIT = 60 << 20
-HANDED = 4
+HANDED = 1
 
 
 def iota(shape, axis):
@@ -186,11 +186,11 @@
     pl.semaphore_wait(ready, Z - 1)
 
     def send_activated(k):
-        if k >= 3:
-            wait_some(send_act.at[k - 3], act_f, Z if k > 3 else Z - 1)
+        if k >= 4:
+            wait_some(send_act.at[k - 4], act_f, Z if k > 4 else Z - 1)
         send_group(k, act_f, st0, me + PAD, send_act.at[k], recv_sem.at[1])
 
-    for k in range(3):
+    for k in range(4):
         send_activated(k)
     st0[me + PAD] = act_f[me]
 
@@ -225,7 +225,7 @@
             device_id={"seq": other * Z + z}, device_id_type=MESH,
         ).start()
     back3[own_frames] = cot_z[:, q]
-    for k in range(3, Q):
+    for k in range(4, Q):
         send_activated(k)
 
     wait_some(recv_sem.at[2], back3, SEQ - Z)
@@ -403,8 +403,9 @@
     wait_some(send_sem.at[0], cot_z, Z - 1)
     wait_all(send_sem.at[1], back0)
     wait_some(send_sem.at[2], back3, SEQ - Z)
+    for k in range(4, Q):
+        wait_some(send_act.at[k], act_f, Z)
     for k in range(5, Q):
-        wait_some(send_act.at[k], act_f, Z)
         wait_some(send_out.at[k], st3, Z)
     wait_some(send_sem.at[3], sum1, PIECES - 1)
     wait_some(send_sem.at[4], sum2, Z // 2 - 1)

time: 115 us -> 115 us (level)
  no operation moved by 1% of the time
where the time goes in v7:
time: 115 us
  Pallas kernels  114 us (99%)
    pallas_call x1, Pallas kernels, body(): pl.pallas_call(functools.partial(kernel, factor), out_shape=(jax.ShapeDty...  112 us

profile of v7, /device:TPU:24, one launch (start us, length us, event | category | flops | bytes accessed | tf_op | source)
XLA Modules:
  0.0 114.6 jit_solution(2663319131604295811)
XLA Ops:
  0.6 111.8 %shard_map.75 = (bf16[1,16,128,128]{3,2,1,0:T(8,128)(2,1)}, bf16[1,16,128,128]{3,2,1,0:T(8,128)(2,1)}, f32[3,3,16,16]{3,2,1,0:T(8,128)}, f32[3,3,16,16]{3,2,1,0:T(8,128)}) custom-call(bf16[1,16,128,128]{3,2,1,0:T(8,128)(2,1)} %clip_hbm.1, bf16[1,16,128,128]{3,2,1,0:T(8,128)(2,1)} %cot_hbm.1, bf16[3,3,16,16]{3,2,1,0:T(8,128)(2,1)} %sw_hbm.1, ...), custom_call_target="tpu_custom_call" | custom-call | tf_op jit(solution)/shard_map/pallas_call | solution.py:442
  112.5 2.1 %shard_map.76 = (bf16[1,16,128,128]{3,2,1,0:T(8,128)(2,1)}, bf16[1,16,128,128]{3,2,1,0:T(8,128)(2,1)}, f32[3,3,16,16]{3,2,1,0:T(8,128)}, f32[3,3,16,16]{3,2,1,0:T(8,128)}) custom-call(bf16[1,16,128,128]{3,2,1,0:T(8,128)(2,1)} %get-tuple-element.8.out_in, bf16[1,16,128,128]{3,2,1,0:T(8,128)(2,1)} %get-tuple-element.9.grad_in, ...), custom_call_target="tpu_custom_call" | custom-call | tf_op jit(solution)/shard_map/pallas_call | solution.py:495

commit v8 on v7

--- a/solution.py
+++ b/solution.py
@@ -85,6 +85,13 @@
     me = lax.axis_index("seq")
     q, z = me // Z, lax.rem(me, Z)
 
+    far_first = sorted(range(1, Z), key=lambda d: -min(d, Z - d))
+    barrier = pltpu.get_barrier_semaphore()
+    for d in far_first:
+        pl.semaphore_signal(barrier, inc=1, device_id={"seq": q * Z + lax.rem(z + d, Z)}, device_id_type=MESH)
+    for d in range(1, Q):
+        pl.semaphore_signal(barrier, inc=1, device_id={"seq": lax.rem(q + d, Q) * Z + z}, device_id_type=MESH)
+
     cot_load = pltpu.make_async_copy(cot_hbm.at[0], cot_in, local_sem.at[0])
     cot_load.start()
     clip_load = pltpu.make_async_copy(clip_hbm.at[0], clip_in, local_sem.at[1])
@@ -94,12 +101,6 @@
     tw_load = pltpu.make_async_copy(tw_hbm, tw_ref, local_sem.at[3])
     tw_load.start()
 
-    barrier = pltpu.get_barrier_semaphore()
-    for d in range(1, Q):
-        pl.semaphore_signal(barrier, inc=1, device_id={"seq": lax.rem(q + d, Q) * Z + z}, device_id_type=MESH)
-    for d in range(1, Z):
-        pl.semaphore_signal(barrier, inc=1, device_id={"seq": q * Z + lax.rem(z + d, Z)}, device_id_type=MESH)
-
     def send_group(k, src, dst, at, sent, received):
         column = lax.rem(q + k, Q) * Z
 
@@ -144,8 +145,7 @@
 
     pl.semaphore_wait(barrier, Q - 1 + Z - 1)
 
-    @pl.loop(1, Z)
-    def _(d):
+    for d in far_first:
         other = lax.rem(z + d, Z)
         pltpu.make_async_remote_copy(
             src_ref=cot_f.at[:, other], dst_ref=cot_z.at[z], send_sem=send_sem.at[0], recv_sem=recv_sem.at[0],

time: 115 us -> 115 us (level)
  no operation moved by 1% of the time
where the time goes in v8:
time: 115 us
  Pallas kernels  114 us (99%)
    pallas_call x1, Pallas kernels, body(): pl.pallas_call(functools.partial(kernel, factor), out_shape=(jax.ShapeDty...  112 us

profile of v8, /device:TPU:24, one launch (start us, length us, event | category | flops | bytes accessed | tf_op | source)
XLA Modules:
  0.0 115.1 jit_solution(8669654837643014785)
XLA Ops:
  0.6 112.3 %shard_map.75 = (bf16[1,16,128,128]{3,2,1,0:T(8,128)(2,1)}, bf16[1,16,128,128]{3,2,1,0:T(8,128)(2,1)}, f32[3,3,16,16]{3,2,1,0:T(8,128)}, f32[3,3,16,16]{3,2,1,0:T(8,128)}) custom-call(bf16[1,16,128,128]{3,2,1,0:T(8,128)(2,1)} %clip_hbm.1, bf16[1,16,128,128]{3,2,1,0:T(8,128)(2,1)} %cot_hbm.1, bf16[3,3,16,16]{3,2,1,0:T(8,128)(2,1)} %sw_hbm.1, ...), custom_call_target="tpu_custom_call" | custom-call | tf_op jit(solution)/shard_map/pallas_call | solution.py:442
  113.0 2.1 %shard_map.76 = (bf16[1,16,128,128]{3,2,1,0:T(8,128)(2,1)}, bf16[1,16,128,128]{3,2,1,0:T(8,128)(2,1)}, f32[3,3,16,16]{3,2,1,0:T(8,128)}, f32[3,3,16,16]{3,2,1,0:T(8,128)}) custom-call(bf16[1,16,128,128]{3,2,1,0:T(8,128)(2,1)} %get-tuple-element.8.out_in, bf16[1,16,128,128]{3,2,1,0:T(8,128)(2,1)} %get-tuple-element.9.grad_in, ...), custom_call_target="tpu_custom_call" | custom-call | tf_op jit(solution)/shard_map/pallas_call | solution.py:495
